TPU v7x, 256 devices: a whole 4x4x8 slice. The times are simulated.
256 devices in a mesh: rep: 8 (over y, x_hi), loop: 32 (over z, x_lo, core).
Axes of the slice: x: 4 (x_hi: 2, x_lo: 2; x = x_hi * 2 + x_lo), y: 4, z: 8, core: 2. Of those that a mesh axis runs over, the one named last changes fastest.
Arguments:
- interactions: int32 [2, 262144, 1024], P(None, ('rep', 'loop')), may hold values from 0 to 3
- user_factors: float32 [262144, 128], P(('rep', 'loop')), may hold values from -2 to 2
- item_factors: float32 [32768, 128], P('loop'), may hold values from -2 to 2
Outputs:
- user_out: float32 [262144, 128], P(('rep', 'loop'))
- item_out: float32 [32768, 128], P('loop')
All inputs are finite; a program needn't handle non-finite values.
Results may differ from a plain program's by a relative error of at most 0.0003.
Values sent between devices are 32-bit elements; how exact they have to be, the bound alone decides.
A program may use at most 64 MiB of HBM per device.

v0:
```python
import jax
import jax.numpy as jnp
from jax import lax
from jax.sharding import PartitionSpec as P

STRATA = 2


ALPHA = 0.5
RATE = 0.01
DECAY = 0.05


def shifted(array, axis, by):
    devices = lax.axis_size(axis)
    return lax.ppermute(array, axis, [(i, (i + by) % devices) for i in range(devices)])


def pass_on(block):
    return shifted(block, "loop", 1)


def body(interactions, user_factors, item_factors):
    hp = lax.Precision.HIGHEST
    users = user_factors
    held = item_factors
    for s in range(STRATA):
        tile = interactions[s]
        conf = 1.0 + ALPHA * tile.astype(jnp.float32)
        pref = (tile > 0).astype(jnp.float32)
        pred = lax.dot_general(users, held, (((1,), (1,)), ((), ())), precision=hp)
        err = conf * (pref - pred)
        last = s + 1 == STRATA
        new_users = users + RATE * (jnp.dot(err, held, precision=hp) - DECAY * users)
        new_items = held + RATE * (
            lax.dot_general(err, users, (((0,), (0,)), ((), ())), precision=hp) - DECAY * held
        )
        users = new_users
        held = new_items if last else pass_on(new_items)
    groups = lax.axis_size("rep")
    averaged = lax.psum(held, "rep") / groups
    return (users, averaged)


def solution(mesh):
    placed = (P(None, ("rep", "loop"), None), P(("rep", "loop"), None), P("loop", None))
    return jax.shard_map(
        body,
        mesh=mesh,
        in_specs=placed,
        out_specs=(P(("rep", "loop"), None), P("loop", None)),
        check_vma=False,
    )
```

profile of v0, /device:TPU:2, one launch (start us, length us, event | category | flops | bytes accessed | tf_op | source)
XLA Modules:
  0.0 148.2 jit_solution(18347875320790705980)
XLA Ops:
  7.2 0.0 copy-start.2
  7.2 0.0 copy-start.1
  7.2 0.0 all-reduce.2.cloned.1.call-start
  7.2 0.0 slice-start
  7.2 7.0 %fusion.1 = f32[1024,1024]{1,0:T(8,128)S(1)} fusion(s32[2,1024,1024]{2,1,0:T(8,128)} %param.3, f32[1024,128]{1,0:T(8,128)} %param.4, f32[1024,128]{1,0:T(8,128)} %param.5), kind=kOutput, calls=%fused_computation.3 | convolution fusion | flops 1617952768 | bytes 9437184 | tf_op jit(solution)/shard_map/dot_general | solution.py:31
  14.2 0.0 copy-done.2
  14.3 0.0 copy-done.1
  14.3 0.0 slice-start.1
  14.3 6.8 %fusion.5 = f32[1024,128]{1,0:T(8,128)S(1)} fusion(f32[1024,128]{1,0:T(8,128)S(1)} %copy-done.2, f32[1024,1024]{1,0:T(8,128)S(1)} %fusion.1, f32[1024,128]{1,0:T(8,128)S(1)} %copy-done.1), kind=kOutput, calls=%fused_computation.10 | convolution fusion | flops 1611137024 | bytes 5767168 | tf_op jit(solution)/shard_map/dot_general | solution.py:36
  21.1 0.3 collective-permute-start
  21.4 3.4 %fusion.3 = f32[1024,128]{1,0:T(8,128)S(1)} fusion(f32[1024,128]{1,0:T(8,128)S(1)} %copy-done.1, f32[1024,1024]{1,0:T(8,128)S(1)} %fusion.1, f32[1024,128]{1,0:T(8,128)S(1)} %copy-done.2), kind=kOutput, calls=%fused_computation.8 | convolution fusion | flops 1611137024 | bytes 5767168 | tf_op jit(solution)/shard_map/dot_general | solution.py:34
  24.8 5.2 %collective-permute-done = f32[1024,128]{1,0:T(8,128)S(1)} collective-permute-done((f32[1024,128]{1,0:T(8,128)S(1)}, f32[1024,128]{1,0:T(8,128)S(1)}, u32[]{:S(2)}, u32[]{:S(2)}) %collective-permute-start) | collective-permute-done | bytes 524320 | tf_op jit(solution)/shard_map/ppermute | solution.py:16
  30.0 0.0 slice-done
  30.0 0.0 slice-done.1
  30.0 4.3 %fusion = f32[1024,1024]{1,0:T(8,128)S(1)} fusion(s32[2,1024,1024]{2,1,0:T(8,128)S(1)} %bitcast.25, f32[1024,128]{1,0:T(8,128)S(1)} %fusion.3, f32[1024,128]{1,0:T(8,128)S(1)} %collective-permute-done), kind=kOutput, calls=%fused_computation.1 | convolution fusion | flops 1617952768 | bytes 9437184 | tf_op jit(solution)/shard_map/dot_general | solution.py:31
  34.3 0.0 copy-start
  34.3 1.9 %copy-done = f32[1024,1024]{1,0:T(8,128)} copy-done((f32[1024,1024]{1,0:T(8,128)}, f32[1024,1024]{1,0:T(8,128)S(1)}, u32[]{:S(2)}) %copy-start) | copy-done | bytes 4194328
  36.2 7.8 %multiply_add_fusion = f32[1024,128]{1,0:T(8,128)} fusion(f32[1024,128]{1,0:T(8,128)S(1)} %collective-permute-done, f32[1024,1024]{1,0:T(8,128)S(1)} %fusion, f32[1024,128]{1,0:T(8,128)S(1)} %fusion.3), kind=kOutput, calls=%fused_computation.13 | convolution fusion | flops 1611137024 | bytes 5767168 | tf_op jit(solution)/shard_map/dot_general | solution.py:36
  44.0 0.0 all-reduce.2.cloned.1.call-update
  44.1 6.4 %fusion.7 = f32[1024,128]{1,0:T(8,128)} fusion(f32[1024,128]{1,0:T(8,128)S(1)} %fusion.3, f32[1024,1024]{1,0:T(8,128)} %copy-done, f32[1024,128]{1,0:T(8,128)S(1)} %collective-permute-done), kind=kOutput, calls=%fused_computation.12 | convolution fusion | flops 1611137024 | bytes 5767168 | tf_op jit(solution)/shard_map/dot_general | solution.py:34
  50.5 89.0 %all-reduce.2.cloned.1.call-done = f32[1024,128]{1,0:T(8,128)} async-done(((f32[1024,128]{1,0:T(8,128)}), f32[1024,128]{1,0:T(8,128)}) %all-reduce.2.cloned.1.call-update) | async-done | bytes 524304 | tf_op jit(solution)/shard_map/psum | solution.py:41
  139.5 1.9 %broadcast_multiply_fusion = f32[1024,128]{1,0:T(8,128)} fusion(f32[1024,128]{1,0:T(8,128)} %all-reduce.2.cloned.1.call-done), kind=kLoop, calls=%fused_computation.14 | loop fusion | flops 131072 | bytes 1048576 | tf_op jit(solution)/shard_map/div | solution.py:41
  (1 shorter events, 0.0 us)
Async XLA Ops:
  7.2 7.1 %copy-start.2 = (f32[1024,128]{1,0:T(8,128)S(1)}, f32[1024,128]{1,0:T(8,128)}, u32[]{:S(2)}) copy-start(f32[1024,128]{1,0:T(8,128)} %param.5) | copy-start | bytes 1572868
  7.2 7.1 %copy-start.1 = (f32[1024,128]{1,0:T(8,128)S(1)}, f32[1024,128]{1,0:T(8,128)}, u32[]{:S(2)}) copy-start(f32[1024,128]{1,0:T(8,128)} %param.4) | copy-start | bytes 1572868
  7.2 132.3 %all-reduce.2.cloned.1.call-start = ((), (), s32[]{:S(2)}) async-start(), calls=%async_computation | async-start | bytes 1048576 | tf_op jit(solution)/shard_map/psum | solution.py:41
  7.2 22.8 %slice-start = ((s8[8388608]{0:T(1024)(128)(4,1)}), s8[4194304]{0:T(1024)(128)(4,1)S(1)}, s32[]{:S(2)}) async-start(s8[8388608]{0:T(1024)(128)(4,1)} %bitcast.24), calls=%async_computation.1 | async-start | bytes 8388608
  14.3 15.7 %slice-start.1 = ((s8[8388608]{0:T(1024)(128)(4,1)}), s8[4194304]{0:T(1024)(128)(4,1)S(1)}, s32[]{:S(2)}) async-start(s8[8388608]{0:T(1024)(128)(4,1)} %bitcast.24), calls=%async_computation.2 | async-start | bytes 8388608
  21.1 8.9 %collective-permute-start = (f32[1024,128]{1,0:T(8,128)S(1)}, f32[1024,128]{1,0:T(8,128)S(1)}, u32[]{:S(2)}, u32[]{:S(2)}) collective-permute-start(f32[1024,128]{1,0:T(8,128)S(1)} %fusion.5), channel_id=1, source_target_pairs={{0,1},{1,2},{2,3},{3,4},{4,5},{5,6},{6,7},{7,8},{8,9},{9,10},{10,1... | collective-permute-start | bytes 1572872 | tf_op jit(solution)/shard_map/ppermute | solution.py:16
  34.3 1.9 %copy-start = (f32[1024,1024]{1,0:T(8,128)}, f32[1024,1024]{1,0:T(8,128)S(1)}, u32[]{:S(2)}) copy-start(f32[1024,1024]{1,0:T(8,128)S(1)} %fusion) | copy-start | bytes 12582916
Sparse Core Ops, SparseCore 0:
  44.2 95.2 all-reduce.1
where the time goes:
time: 149 us; the launch traced here: 148 us
  waiting for transfers between devices  94.2 us (63%)
  matrix products  35.7 us (24%)
  between operations  14.1 us (9%)
  local copies, waits for them, and re-layouts  1.95 us (1%)
  other arithmetic  1.87 us (1%)
    psum x1, waiting for transfers between devices, body(): averaged = lax.psum(held, 'rep') / groups  89 us
    dot_general x2, matrix products, body(): lax.dot_general(err, users, (((0,), (0,)), ((), ())), precision=hp)  14.7 us
    dot_general x2, matrix products, body(): pred = lax.dot_general(users, held, (((1,), (1,)), ((), ())), precision=hp)  11.3 us
    dot_general x2, matrix products, body(): jnp.dot(err, held, precision=hp) - DECAY * users  9.82 us
    ppermute x1, waiting for transfers between devices, shifted(): lax.ppermute(array, axis, [(i, (i + by) % devices) for i in range(devices)])  5.16 us
  transfers between devices with their start and end apart: 2, of which 2 were waited for; matrix products, arithmetic and copies ran while one was open for 7% of the time, Pallas kernels for 0%

commit v1 on v0

v1 whole, which is shorter than its diff:
```python
import functools

import jax
import jax.numpy as jnp
from jax import lax
from jax.experimental import pallas as pl
from jax.experimental.pallas import tpu as pltpu
from jax.sharding import PartitionSpec as P

ALPHA = 0.5
RATE = 0.01
DECAY = 0.05
KEEP = 1.0 - RATE * DECAY
STEP = RATE * ALPHA
N = 1024
R = 128
CHUNK = 256
CHUNKS = N // CHUNK
ROWS = 256
REPS = 8
PIECE = CHUNK // REPS
OTHERS = [(2, 1), (1, 1), (3, 1), (2, 0), (0, 1), (1, 0), (3, 0)]
MESH = pl.DeviceIdType.MESH
F32 = jnp.float32
BF16 = jnp.bfloat16
NT = (((1,), (1,)), ((), ()))
NN = (((1,), (0,)), ((), ()))


def split(x):
    hi = x.astype(BF16)
    return hi, (x - hi.astype(F32)).astype(BF16)


def dot(a, b, dims):
    return lax.dot_general(a, b, dims, preferred_element_type=F32)


def kernel(comm, inter, users, items, user_out, item_out, tile, uv, held0, held1, sent0, sent1,
           ucat, utcat, hpred, hnew, ghi, glo, parts, mean,
           in_sem, tile_sem, out_sem, own_sem, ring_send, ring_recv, rs_send, rs_recv, ag_send, ag_recv):
    if comm:
        rep = lax.axis_index("rep")
        loop = lax.axis_index("loop")
        y, xh = rep // 2, rep % 2
        after = (rep, (loop + 1) % 32)
        before = (rep, (loop + 31) % 32)
        ranks_to = [((y + a) % 4) * 2 + (xh + b) % 2 for a, b in OTHERS]
        ranks_from = [((y + 4 - a) % 4) * 2 + (xh + b) % 2 for a, b in OTHERS]
        barrier = pltpu.get_barrier_semaphore()
        pl.semaphore_signal(barrier, inc=1, device_id=before, device_id_type=MESH)
        for k in range(len(OTHERS)):
            pl.semaphore_signal(barrier, inc=1, device_id=(ranks_from[k], loop), device_id_type=MESH)
    else:
        rep = 0

    loads = [pltpu.make_async_copy(users, uv, in_sem.at[0]), pltpu.make_async_copy(items, held0, in_sem.at[1])]
    for c in loads:
        c.start()
    tiles = []
    for s in range(2):
        for c in range(CHUNKS):
            cols = pl.ds(c * CHUNK, CHUNK)
            t = pltpu.make_async_copy(inter.at[s, :, cols], tile.at[s, :, cols], tile_sem.at[s, c])
            t.start()
            tiles.append(t)
    for c in loads:
        c.wait()

    ring = []
    scatter = []
    gather = []
    outs = []
    for s in range(2):
        held = held0 if s == 0 else held1
        sent = sent0 if s == 0 else sent1
        for u in range(N // ROWS):
            rows = pl.ds(u * ROWS, ROWS)
            block = uv[rows, :]
            hi, lo = split(block)
            ucat[rows, 0:R] = hi
            ucat[rows, R:2 * R] = lo
            hi, lo = split(block.T)
            utcat[0:R, rows] = hi
            utcat[R:2 * R, rows] = lo
        for c in range(CHUNKS):
            cols = pl.ds(c * CHUNK, CHUNK)
            if s == 1 and comm:
                ring[c].wait_recv()
            h = held[cols, :]
            hi, lo = split(h)
            hnew[cols, 0:R] = hi
            hnew[cols, R:2 * R] = lo
            hpred[:, 0:R] = hi
            hpred[:, R:2 * R] = hi
            hpred[:, 2 * R:3 * R] = lo
            hpred[:, 3 * R:4 * R] = lo
            tiles[s * CHUNKS + c].wait()
            for u in range(N // ROWS):
                rows = pl.ds(u * ROWS, ROWS)
                uc = ucat[rows, :]
                pred = dot(uc, hpred[:, 0:2 * R], NT) + dot(uc, hpred[:, 2 * R:4 * R], NT)
                t = tile[s, rows, cols].astype(F32)
                hi, lo = split((1.0 / ALPHA + t) * (jnp.minimum(t, 1.0) - pred))
                ghi[rows, cols] = hi
                glo[rows, cols] = lo
            d = dot(utcat[...], ghi[:, cols], NN) + dot(utcat[...], glo[:, cols], NN)
            new = KEEP * h + STEP * (d[0:R] + d[R:2 * R]).T
            sent[cols, :] = new
            if not comm:
                if s == 0:
                    held1[cols, :] = new
                else:
                    o = pltpu.make_async_copy(sent1.at[cols], item_out.at[cols], own_sem.at[c])
                    o.start()
                    outs.append(o)
                continue
            if s == 0:
                if c == 0:
                    pl.semaphore_wait(barrier, 1 + len(OTHERS))
                cp = pltpu.make_async_remote_copy(
                    src_ref=sent0.at[cols], dst_ref=held1.at[cols],
                    send_sem=ring_send.at[c], recv_sem=ring_recv.at[c],
                    device_id=after, device_id_type=MESH)
                cp.start()
                ring.append(cp)
            else:
                group = []
                for k in range(len(OTHERS)):
                    at = pl.multiple_of(c * CHUNK + ranks_to[k] * PIECE, PIECE)
                    cp = pltpu.make_async_remote_copy(
                        src_ref=sent1.at[pl.ds(at, PIECE)], dst_ref=parts.at[c, k],
                        send_sem=rs_send.at[c, k], recv_sem=rs_recv.at[c, k],
                        device_id=(ranks_to[k], loop), device_id_type=MESH)
                    cp.start()
                    group.append(cp)
                scatter.append(group)

        def finish(c):
            mine = pl.ds(pl.multiple_of(c * CHUNK + rep * PIECE, PIECE), PIECE)
            for cp in scatter[c]:
                cp.wait_recv()
            total = sent1[mine, :]
            for k in range(len(OTHERS)):
                total = total + parts[c, k]
            mean[c] = total * (1.0 / REPS)
            own = pltpu.make_async_copy(mean.at[c], item_out.at[mine], own_sem.at[c])
            own.start()
            outs.append(own)
            group = []
            for k in range(len(OTHERS)):
                cp = pltpu.make_async_remote_copy(
                    src_ref=mean.at[c], dst_ref=item_out.at[mine],
                    send_sem=ag_send.at[c, k], recv_sem=ag_recv.at[c, k],
                    device_id=(ranks_to[k], loop), device_id_type=MESH)
                cp.start()
                group.append(cp)
            gather.append(group)

        for u in range(N // ROWS):
            rows = pl.ds(u * ROWS, ROWS)
            d = dot(ghi[rows, :], hnew[...], NN) + dot(glo[rows, :], hnew[...], NN)
            uv[rows, :] = KEEP * uv[rows, :] + STEP * (d[:, 0:R] + d[:, R:2 * R])
            if s == 1:
                o = pltpu.make_async_copy(uv.at[rows], user_out.at[rows], out_sem.at[u])
                o.start()
                outs.append(o)
                if comm and u < CHUNKS:
                    finish(u)
    if comm:
        for cp in ring:
            cp.wait_send()
        for group in scatter:
            for cp in group:
                cp.wait_send()
        for group in gather:
            for cp in group:
                cp.wait_send()
                cp.wait_recv()
    for o in outs:
        o.wait()


def body(interactions, user_factors, item_factors, comm=True):
    n = len(OTHERS)
    return pl.pallas_call(
        functools.partial(kernel, comm),
        out_shape=[jax.ShapeDtypeStruct((N, R), F32)] * 2,
        in_specs=[pl.BlockSpec(memory_space=pl.ANY)] * 3,
        out_specs=[pl.BlockSpec(memory_space=pl.ANY)] * 2,
        scratch_shapes=[
            pltpu.VMEM((2, N, N), jnp.int32),
            pltpu.VMEM((N, R), F32),
            pltpu.VMEM((N, R), F32),
            pltpu.VMEM((N, R), F32),
            pltpu.VMEM((N, R), F32),
            pltpu.VMEM((N, R), F32),
            pltpu.VMEM((N, 2 * R), BF16),
            pltpu.VMEM((2 * R, N), BF16),
            pltpu.VMEM((CHUNK, 4 * R), BF16),
            pltpu.VMEM((N, 2 * R), BF16),
            pltpu.VMEM((N, N), BF16),
            pltpu.VMEM((N, N), BF16),
            pltpu.VMEM((CHUNKS, n, PIECE, R), F32),
            pltpu.VMEM((CHUNKS, PIECE, R), F32),
            pltpu.SemaphoreType.DMA((2,)),
            pltpu.SemaphoreType.DMA((2, CHUNKS)),
            pltpu.SemaphoreType.DMA((N // ROWS,)),
            pltpu.SemaphoreType.DMA((CHUNKS,)),
            pltpu.SemaphoreType.DMA((CHUNKS,)),
            pltpu.SemaphoreType.DMA((CHUNKS,)),
            pltpu.SemaphoreType.DMA((CHUNKS, n)),
            pltpu.SemaphoreType.DMA((CHUNKS, n)),
            pltpu.SemaphoreType.DMA((CHUNKS, n)),
            pltpu.SemaphoreType.DMA((CHUNKS, n)),
        ],
        name="sgd_window",
        compiler_params=pltpu.CompilerParams(
            collective_id=0 if comm else None, has_side_effects=True, vmem_limit_bytes=60 << 20
        ),
    )(interactions, user_factors, item_factors)


def solution(mesh):
    placed = (P(None, ("rep", "loop"), None), P(("rep", "loop"), None), P("loop", None))
    return jax.shard_map(
        body,
        mesh=mesh,
        in_specs=placed,
        out_specs=(P(("rep", "loop"), None), P("loop", None)),
        check_vma=False,
    )
```

time: 149 us -> 38 us (0.26)
  waiting for transfers between devices: 94.2 us -> 0 us
  matrix products: 35.7 us -> 0 us
  Pallas kernels: 0 us -> 33.4 us
  between operations: 14.1 us -> 0.64 us
  other arithmetic: 1.87 us -> 0 us
  local copies, waits for them, and re-layouts: 1.95 us -> 3.74 us
    psum x1 -> x0, waiting for transfers between devices: 89 us -> none  [body(): averaged = lax.psum(held, 'rep') / groups]
    dot_general x6 -> x0, matrix products: 35.7 us -> none  [the longest x2 14.7 us: body(): lax.dot_general(err, users, (((0,), (0,)), ((), ())), precision=hp)]
    pallas_call x0 -> x1, Pallas kernels: none -> 33.4 us  [body(): pl.pallas_call(functools.partial(kernel, comm), out_shape=[jax.ShapeDtype...]
    ppermute x1 -> x0, waiting for transfers between devices: 5.16 us -> none  [shifted(): lax.ppermute(array, axis, [(i, (i + by) % devices) for i in range(devices)])]
    div x1 -> x0, other arithmetic: 1.87 us -> none  [body(): averaged = lax.psum(held, 'rep') / groups]
    unnamed x10 -> x2, local copies, waits for them, and re-layouts: 1.95 us -> 3.74 us
  transfers between devices with their start and end apart: 2 -> 0, of which waited for: 2 -> 0; matrix products, arithmetic and copies ran while one was open for 7% -> 0% of each run, Pallas kernels for 0% -> 0%
where the time goes in v1:
time: 38 us; the launch traced here: 37.8 us
  Pallas kernels  33.4 us (88%)
  local copies, waits for them, and re-layouts  3.74 us (10%)
  between operations  0.64 us (2%)
    pallas_call x1, Pallas kernels, body(): pl.pallas_call(functools.partial(kernel, comm), out_shape=[jax.ShapeDtype...  33.4 us
    unnamed x2, local copies, waits for them, and re-layouts  3.74 us

profile of v1, /device:TPU:2, one launch (start us, length us, event | category | flops | bytes accessed | tf_op | source)
XLA Modules:
  0.0 37.8 jit_solution(9240349523732618847)
XLA Ops:
  0.6 33.4 %sgd_window.1 = (f32[1024,128]{1,0:T(8,128)}, f32[1024,128]{1,0:T(8,128)}) custom-call(s32[2,1024,1024]{2,1,0:T(8,128)} %inter.1, f32[1024,128]{1,0:T(8,128)} %users.1, f32[1024,128]{1,0:T(8,128)} %items.1), custom_call_target="tpu_custom_call" | custom-call | tf_op jit(solution)/shard_map/sgd_window/pallas_call | solution.py:186
  34.1 1.9 %copy.7 = f32[1024,128]{1,0:T(8,128)} copy(f32[1024,128]{1,0:T(8,128)} %get-tuple-element.4) | data formatting | bytes 1048576
  35.9 1.9 %copy.8 = f32[1024,128]{1,0:T(8,128)} copy(f32[1024,128]{1,0:T(8,128)} %get-tuple-element.5) | data formatting | bytes 1048576

commit v2 on v1

--- a/solution.py
+++ b/solution.py
@@ -15,8 +15,12 @@
 N = 1024
 R = 128
 CHUNK = 256
+PARTS = 2
 CHUNKS = N // CHUNK
 ROWS = 256
+DROWS = 256
+KCAT = 1
+SKEW = 1
 REPS = 8
 PIECE = CHUNK // REPS
 OTHERS = [(2, 1), (1, 1), (3, 1), (2, 0), (0, 1), (1, 0), (3, 0)]
@@ -37,7 +41,7 @@
 
 
 def kernel(comm, inter, users, items, user_out, item_out, tile, uv, held0, held1, sent0, sent1,
-           ucat, utcat, hpred, hnew, ghi, glo, parts, mean,
+           ucat, utcat, hpred, hnew, ghi, glo, acc, parts, mean,
            in_sem, tile_sem, out_sem, own_sem, ring_send, ring_recv, rs_send, rs_recv, ag_send, ag_recv):
     if comm:
         rep = lax.axis_index("rep")
@@ -59,10 +63,11 @@
         c.start()
     tiles = []
     for s in range(2):
-        for c in range(CHUNKS):
-            cols = pl.ds(c * CHUNK, CHUNK)
-            t = pltpu.make_async_copy(inter.at[s, :, cols], tile.at[s, :, cols], tile_sem.at[s, c])
-            t.start()
+        for u in range(N // ROWS):
+            rows = pl.ds(u * ROWS, ROWS)
+            t = pltpu.make_async_copy(inter.at[s, rows], tile.at[s, rows], tile_sem.at[s, u])
+            if s == 0:
+                t.start()
             tiles.append(t)
     for c in loads:
         c.wait()
@@ -80,32 +85,54 @@
             hi, lo = split(block)
             ucat[rows, 0:R] = hi
             ucat[rows, R:2 * R] = lo
-            hi, lo = split(block.T)
+
+        def turn(u):
+            rows = pl.ds(u * ROWS, ROWS)
+            hi, lo = split(uv[rows, :].T)
             utcat[0:R, rows] = hi
             utcat[R:2 * R, rows] = lo
-        for c in range(CHUNKS):
+
+        def prepare(c):
             cols = pl.ds(c * CHUNK, CHUNK)
-            if s == 1 and comm:
-                ring[c].wait_recv()
             h = held[cols, :]
             hi, lo = split(h)
             hnew[cols, 0:R] = hi
             hnew[cols, R:2 * R] = lo
-            hpred[:, 0:R] = hi
-            hpred[:, R:2 * R] = hi
-            hpred[:, 2 * R:3 * R] = lo
-            hpred[:, 3 * R:4 * R] = lo
-            tiles[s * CHUNKS + c].wait()
-            for u in range(N // ROWS):
-                rows = pl.ds(u * ROWS, ROWS)
-                uc = ucat[rows, :]
-                pred = dot(uc, hpred[:, 0:2 * R], NT) + dot(uc, hpred[:, 2 * R:4 * R], NT)
-                t = tile[s, rows, cols].astype(F32)
-                hi, lo = split((1.0 / ALPHA + t) * (jnp.minimum(t, 1.0) - pred))
-                ghi[rows, cols] = hi
-                glo[rows, cols] = lo
-            d = dot(utcat[...], ghi[:, cols], NN) + dot(utcat[...], glo[:, cols], NN)
-            new = KEEP * h + STEP * (d[0:R] + d[R:2 * R]).T
+            hi, lo = split(h.T)
+            hpred[0:R, cols] = hi
+            hpred[R:2 * R, cols] = hi
+            hpred[2 * R:3 * R, cols] = lo
+            hpred[3 * R:4 * R, cols] = lo
+
+        def errors(c, u):
+            cols = pl.ds(c * CHUNK, CHUNK)
+            rows = pl.ds(u * ROWS, ROWS)
+            uc = ucat[rows, :]
+            if KCAT:
+                pred = dot(jnp.concatenate([uc, uc], 1), hpred[:, cols], NN)
+            else:
+                pred = dot(uc, hpred[0:2 * R, cols], NN) + dot(uc, hpred[2 * R:4 * R, cols], NN)
+            t = tile[s, rows, cols].astype(F32)
+            hi, lo = split((1.0 / ALPHA + t) * (jnp.minimum(t, 1.0) - pred))
+            ghi[rows, cols] = hi
+            glo[rows, cols] = lo
+
+        def gradient(c, u):
+            cols = pl.ds(c * CHUNK, CHUNK)
+            rows = pl.ds(u * DROWS, DROWS)
+            ut = utcat[:, rows]
+            if KCAT:
+                d = dot(jnp.concatenate([ut, ut], 1), jnp.concatenate([ghi[rows, cols], glo[rows, cols]], 0), NN)
+            else:
+                d = dot(ut, ghi[rows, cols], NN) + dot(ut, glo[rows, cols], NN)
+            if u == 0:
+                acc[...] = d
+            else:
+                acc[...] += d
+
+        def update(c):
+            cols = pl.ds(c * CHUNK, CHUNK)
+            new = KEEP * held[cols, :] + STEP * (acc[0:R, :] + acc[R:2 * R, :]).T
             sent[cols, :] = new
             if not comm:
                 if s == 0:
@@ -114,7 +141,7 @@
                     o = pltpu.make_async_copy(sent1.at[cols], item_out.at[cols], own_sem.at[c])
                     o.start()
                     outs.append(o)
-                continue
+                return
             if s == 0:
                 if c == 0:
                     pl.semaphore_wait(barrier, 1 + len(OTHERS))
@@ -136,6 +163,44 @@
                     group.append(cp)
                 scatter.append(group)
 
+        if s == 0:
+            prepare(0)
+        if s == 0 and SKEW:
+            for u in range(N // ROWS):
+                tiles[u].wait()
+                errors(0, u)
+                turn(u)
+            for t in tiles[N // ROWS:]:
+                t.start()
+            for c in range(1, CHUNKS):
+                prepare(c)
+                for u in range(N // ROWS):
+                    errors(c, u)
+                    if ROWS == DROWS:
+                        gradient(c - 1, u)
+                if ROWS != DROWS:
+                    for u in range(N // DROWS):
+                        gradient(c - 1, u)
+                update(c - 1)
+            for u in range(N // DROWS):
+                gradient(CHUNKS - 1, u)
+            update(CHUNKS - 1)
+        else:
+            for c in range(CHUNKS):
+                if s == 1 and comm:
+                    ring[c].wait_recv()
+                if s == 1 or c > 0:
+                    prepare(c)
+                for u in range(N // ROWS):
+                    if c == 0:
+                        tiles[s * (N // ROWS) + u].wait()
+                    errors(c, u)
+                    if c == 0:
+                        turn(u)
+                for u in range(N // DROWS):
+                    gradient(c, u)
+                update(c)
+
         def finish(c):
             mine = pl.ds(pl.multiple_of(c * CHUNK + rep * PIECE, PIECE), PIECE)
             for cp in scatter[c]:
@@ -181,9 +246,27 @@
         o.wait()
 
 
+def place(users, items, user_out, item_out, buf, in_sem, out_sem):
+    rows = [pl.ds(p * (N // PARTS), N // PARTS) for p in range(PARTS)]
+    ins, outs = [], []
+    for a, src in enumerate((users, items)):
+        for p in range(PARTS):
+            cp = pltpu.make_async_copy(src.at[rows[p]], buf.at[a, rows[p]], in_sem.at[a, p])
+            cp.start()
+            ins.append(cp)
+    for a, dst in enumerate((user_out, item_out)):
+        for p in range(PARTS):
+            ins[a * PARTS + p].wait()
+            cp = pltpu.make_async_copy(buf.at[a, rows[p]], dst.at[rows[p]], out_sem.at[a, p])
+            cp.start()
+            outs.append(cp)
+    for cp in outs:
+        cp.wait()
+
+
 def body(interactions, user_factors, item_factors, comm=True):
     n = len(OTHERS)
-    return pl.pallas_call(
+    users, items = pl.pallas_call(
         functools.partial(kernel, comm),
         out_shape=[jax.ShapeDtypeStruct((N, R), F32)] * 2,
         in_specs=[pl.BlockSpec(memory_space=pl.ANY)] * 3,
@@ -197,14 +280,15 @@
             pltpu.VMEM((N, R), F32),
             pltpu.VMEM((N, 2 * R), BF16),
             pltpu.VMEM((2 * R, N), BF16),
-            pltpu.VMEM((CHUNK, 4 * R), BF16),
+            pltpu.VMEM((4 * R, N), BF16),
             pltpu.VMEM((N, 2 * R), BF16),
             pltpu.VMEM((N, N), BF16),
             pltpu.VMEM((N, N), BF16),
+            pltpu.VMEM((2 * R, CHUNK), F32),
             pltpu.VMEM((CHUNKS, n, PIECE, R), F32),
             pltpu.VMEM((CHUNKS, PIECE, R), F32),
             pltpu.SemaphoreType.DMA((2,)),
-            pltpu.SemaphoreType.DMA((2, CHUNKS)),
+            pltpu.SemaphoreType.DMA((2, N // ROWS)),
             pltpu.SemaphoreType.DMA((N // ROWS,)),
             pltpu.SemaphoreType.DMA((CHUNKS,)),
             pltpu.SemaphoreType.DMA((CHUNKS,)),
@@ -219,6 +303,21 @@
             collective_id=0 if comm else None, has_side_effects=True, vmem_limit_bytes=60 << 20
         ),
     )(interactions, user_factors, item_factors)
+    if not comm:
+        return users, items
+    return pl.pallas_call(
+        place,
+        out_shape=[jax.ShapeDtypeStruct((N, R), F32)] * 2,
+        in_specs=[pl.BlockSpec(memory_space=pl.ANY)] * 2,
+        out_specs=[pl.BlockSpec(memory_space=pl.ANY)] * 2,
+        scratch_shapes=[
+            pltpu.VMEM((2, N, R), F32),
+            pltpu.SemaphoreType.DMA((2, PARTS)),
+            pltpu.SemaphoreType.DMA((2, PARTS)),
+        ],
+        name="place",
+        compiler_params=pltpu.CompilerParams(vmem_limit_bytes=60 << 20),
+    )(users, items)
 
 
 def solution(mesh):

time: 38 us -> 35.2 us (0.926)
  local copies, waits for them, and re-layouts: 3.74 us -> 0 us
  Pallas kernels: 33.4 us -> 34.4 us
    unnamed x2 -> x0, local copies, waits for them, and re-layouts: 3.74 us -> none
    pallas_call x0 -> x1, Pallas kernels: none -> 1.98 us  [body(): pl.pallas_call(place, out_shape=[jax.ShapeDtypeStruct((N, R), F32)] * 2,...]
    pallas_call x1, Pallas kernels: 33.4 us -> 32.5 us  [body(): pl.pallas_call(functools.partial(kernel, comm), out_shape=[jax.ShapeDtype...]
where the time goes in v2:
time: 35.2 us; the launch traced here: 35.1 us
  Pallas kernels  34.4 us (98%)
  between operations  0.64 us (2%)
    pallas_call x1, Pallas kernels, body(): pl.pallas_call(functools.partial(kernel, comm), out_shape=[jax.ShapeDtype...  32.5 us
    pallas_call x1, Pallas kernels, body(): pl.pallas_call(place, out_shape=[jax.ShapeDtypeStruct((N, R), F32)] * 2,...  1.98 us

profile of v2, /device:TPU:2, one launch (start us, length us, event | category | flops | bytes accessed | tf_op | source)
XLA Modules:
  0.0 35.1 jit_solution(9685963431855193375)
XLA Ops:
  0.6 32.5 %sgd_window.1 = (f32[1024,128]{1,0:T(8,128)}, f32[1024,128]{1,0:T(8,128)}) custom-call(s32[2,1024,1024]{2,1,0:T(8,128)} %inter.1, f32[1024,128]{1,0:T(8,128)} %users.1, f32[1024,128]{1,0:T(8,128)} %items.1), custom_call_target="tpu_custom_call" | custom-call | tf_op jit(solution)/shard_map/sgd_window/pallas_call | solution.py:269
  33.1 2.0 %place.1 = (f32[1024,128]{1,0:T(8,128)}, f32[1024,128]{1,0:T(8,128)}) custom-call(f32[1024,128]{1,0:T(8,128)} %get-tuple-element.4.users, f32[1024,128]{1,0:T(8,128)} %get-tuple-element.5.items), custom_call_target="tpu_custom_call" | custom-call | tf_op jit(solution)/shard_map/place/pallas_call | solution.py:308

commit v3 on v2

--- a/solution.py
+++ b/solution.py
@@ -19,6 +19,11 @@
 CHUNKS = N // CHUNK
 ROWS = 256
 DROWS = 256
+STEPS = (2, 1, 3)
+PAIRED_EARLY = [[], [], [], [(0, 0), (0, 1)]]
+PAIRED_ORDER = [[], [(0, 2), (0, 3), (1, 0), (1, 1)], [], [(1, 2), (1, 3)]]
+DIRECT_EARLY = [[], [], [], []]
+DIRECT_ORDER = [[(2, 0)], [(2, 1)], [(2, 2)], [(2, 3)]]
 KCAT = 1
 SKEW = 1
 REPS = 8
@@ -41,12 +46,14 @@
 
 
 def kernel(comm, inter, users, items, user_out, item_out, tile, uv, held0, held1, sent0, sent1,
-           ucat, utcat, hpred, hnew, ghi, glo, acc, parts, mean,
-           in_sem, tile_sem, out_sem, own_sem, ring_send, ring_recv, rs_send, rs_recv, ag_send, ag_recv):
+           ucat, utcat, hpred, hnew, ghi, glo, acc, parts, pairs, pair, other, mean,
+           in_sem, tile_sem, out_sem, own_sem, ring_send, ring_recv, rs_send, rs_recv, x_send, x_recv, ag_send, ag_recv):
     if comm:
         rep = lax.axis_index("rep")
         loop = lax.axis_index("loop")
         y, xh = rep // 2, rep % 2
+        across = (y * 2 + 1 - xh, loop)
+        paired = loop // 2 % 2 == 1
         after = (rep, (loop + 1) % 32)
         before = (rep, (loop + 31) % 32)
         ranks_to = [((y + a) % 4) * 2 + (xh + b) % 2 for a, b in OTHERS]
@@ -73,9 +80,76 @@
         c.wait()
 
     ring = []
-    scatter = []
-    gather = []
     outs = []
+    def remote(src, dst, send_sem, recv_sem, to):
+        return pltpu.make_async_remote_copy(
+            src_ref=src, dst_ref=dst, send_sem=send_sem, recv_sem=recv_sem,
+            device_id=to, device_id_type=MESH)
+
+    def rows_of(c, i, size):
+        return pl.ds(pl.multiple_of(c * CHUNK + i * size, size), size)
+
+    def scatter(c, k):
+        return remote(sent1.at[rows_of(c, ranks_to[k], PIECE)], parts.at[c, k],
+                      rs_send.at[c, k], rs_recv.at[c, k], (ranks_to[k], loop))
+
+    def gather(c, k):
+        return remote(mean.at[c, pl.ds(0, PIECE)], item_out.at[rows_of(c, rep, PIECE)],
+                      ag_send.at[c, k], ag_recv.at[c, k], (ranks_to[k], loop))
+
+    def scatter_pair(c, k):
+        to = (y + STEPS[k]) % 4
+        return remote(sent1.at[rows_of(c, to, 2 * PIECE)], pairs.at[c, k],
+                      rs_send.at[c, k], rs_recv.at[c, k], (to * 2 + xh, loop))
+
+    def swap_pair(c):
+        return remote(pair.at[c], other.at[c], x_send.at[c], x_recv.at[c], across)
+
+    def gather_pair(c, k):
+        return remote(mean.at[c], item_out.at[rows_of(c, y, 2 * PIECE)],
+                      ag_send.at[c, k], ag_recv.at[c, k], ((y + STEPS[k]) % 4 * 2 + xh, loop))
+
+    def own_pair(c):
+        return pltpu.make_async_copy(mean.at[c], item_out.at[rows_of(c, y, 2 * PIECE)], own_sem.at[c])
+
+    def own(c):
+        return pltpu.make_async_copy(mean.at[c, pl.ds(0, PIECE)], item_out.at[rows_of(c, rep, PIECE)], own_sem.at[c])
+
+    def along_y(c):
+        for k in range(len(STEPS)):
+            scatter_pair(c, k).wait_recv()
+        total = sent1[rows_of(c, y, 2 * PIECE), :]
+        for k in range(len(STEPS)):
+            total = total + pairs[c, k]
+        pair[c] = total
+        swap_pair(c).start()
+
+    def along_x(c):
+        swap_pair(c).wait_recv()
+        mean[c] = (pair[c] + other[c]) * (1.0 / REPS)
+        for k in range(len(STEPS)):
+            gather_pair(c, k).start()
+        own_pair(c).start()
+
+    def finish(c):
+        for k in range(len(OTHERS)):
+            scatter(c, k).wait_recv()
+        total = sent1[rows_of(c, rep, PIECE), :]
+        for k in range(len(OTHERS)):
+            total = total + parts[c, k]
+        mean[c, 0:PIECE] = total * (1.0 / REPS)
+        for k in range(len(OTHERS)):
+            gather(c, k).start()
+        own(c).start()
+
+    def go_on(pairwise, straight):
+        for on, stages in ((paired, pairwise), (jnp.logical_not(paired), straight)):
+            if stages:
+                @pl.when(on)
+                def _():
+                    for stage, c in stages:
+                        (along_y, along_x, finish)[stage](c)
+
     for s in range(2):
         held = held0 if s == 0 else held1
         sent = sent0 if s == 0 else sent1
@@ -152,16 +226,15 @@
                 cp.start()
                 ring.append(cp)
             else:
-                group = []
-                for k in range(len(OTHERS)):
-                    at = pl.multiple_of(c * CHUNK + ranks_to[k] * PIECE, PIECE)
-                    cp = pltpu.make_async_remote_copy(
-                        src_ref=sent1.at[pl.ds(at, PIECE)], dst_ref=parts.at[c, k],
-                        send_sem=rs_send.at[c, k], recv_sem=rs_recv.at[c, k],
-                        device_id=(ranks_to[k], loop), device_id_type=MESH)
-                    cp.start()
-                    group.append(cp)
-                scatter.append(group)
+                @pl.when(paired)
+                def _():
+                    for k in range(len(STEPS)):
+                        scatter_pair(c, k).start()
+
+                @pl.when(jnp.logical_not(paired))
+                def _():
+                    for k in range(len(OTHERS)):
+                        scatter(c, k).start()
 
         if s == 0:
             prepare(0)
@@ -200,27 +273,8 @@
                 for u in range(N // DROWS):
                     gradient(c, u)
                 update(c)
-
-        def finish(c):
-            mine = pl.ds(pl.multiple_of(c * CHUNK + rep * PIECE, PIECE), PIECE)
-            for cp in scatter[c]:
-                cp.wait_recv()
-            total = sent1[mine, :]
-            for k in range(len(OTHERS)):
-                total = total + parts[c, k]
-            mean[c] = total * (1.0 / REPS)
-            own = pltpu.make_async_copy(mean.at[c], item_out.at[mine], own_sem.at[c])
-            own.start()
-            outs.append(own)
-            group = []
-            for k in range(len(OTHERS)):
-                cp = pltpu.make_async_remote_copy(
-                    src_ref=mean.at[c], dst_ref=item_out.at[mine],
-                    send_sem=ag_send.at[c, k], recv_sem=ag_recv.at[c, k],
-                    device_id=(ranks_to[k], loop), device_id_type=MESH)
-                cp.start()
-                group.append(cp)
-            gather.append(group)
+                if comm and s == 1:
+                    go_on(PAIRED_EARLY[c], DIRECT_EARLY[c])
 
         for u in range(N // ROWS):
             rows = pl.ds(u * ROWS, ROWS)
@@ -230,18 +284,29 @@
                 o = pltpu.make_async_copy(uv.at[rows], user_out.at[rows], out_sem.at[u])
                 o.start()
                 outs.append(o)
-                if comm and u < CHUNKS:
-                    finish(u)
+                if comm:
+                    go_on(PAIRED_ORDER[u], DIRECT_ORDER[u])
     if comm:
         for cp in ring:
             cp.wait_send()
-        for group in scatter:
-            for cp in group:
-                cp.wait_send()
-        for group in gather:
-            for cp in group:
-                cp.wait_send()
-                cp.wait_recv()
+
+        @pl.when(paired)
+        def _():
+            for c in range(CHUNKS):
+                swap_pair(c).wait_send()
+                own_pair(c).wait()
+                for k in range(len(STEPS)):
+                    scatter_pair(c, k).wait_send()
+                    gather_pair(c, k).wait()
+
+        @pl.when(jnp.logical_not(paired))
+        def _():
+            for c in range(CHUNKS):
+                own(c).wait()
+                for k in range(len(OTHERS)):
+                    scatter(c, k).wait_send()
+                    gather(c, k).wait()
+
     for o in outs:
         o.wait()
 
@@ -286,7 +351,10 @@
             pltpu.VMEM((N, N), BF16),
             pltpu.VMEM((2 * R, CHUNK), F32),
             pltpu.VMEM((CHUNKS, n, PIECE, R), F32),
-            pltpu.VMEM((CHUNKS, PIECE, R), F32),
+            pltpu.VMEM((CHUNKS, len(STEPS), 2 * PIECE, R), F32),
+            pltpu.VMEM((CHUNKS, 2 * PIECE, R), F32),
+            pltpu.VMEM((CHUNKS, 2 * PIECE, R), F32),
+            pltpu.VMEM((CHUNKS, 2 * PIECE, R), F32),
             pltpu.SemaphoreType.DMA((2,)),
             pltpu.SemaphoreType.DMA((2, N // ROWS)),
             pltpu.SemaphoreType.DMA((N // ROWS,)),
@@ -295,6 +363,8 @@
             pltpu.SemaphoreType.DMA((CHUNKS,)),
             pltpu.SemaphoreType.DMA((CHUNKS, n)),
             pltpu.SemaphoreType.DMA((CHUNKS, n)),
+            pltpu.SemaphoreType.DMA((CHUNKS,)),
+            pltpu.SemaphoreType.DMA((CHUNKS,)),
             pltpu.SemaphoreType.DMA((CHUNKS, n)),
             pltpu.SemaphoreType.DMA((CHUNKS, n)),
         ],

time: 35.2 us -> 33.2 us (0.943)
  the two profiles are of different devices: /device:TPU:2 before, /device:TPU:8 now
where the time goes in v3:
time: 33.2 us; the launch traced here: 33.1 us
  Pallas kernels  32.5 us (98%)
  between operations  0.64 us (2%)
    pallas_call x1, Pallas kernels, body(): pl.pallas_call(functools.partial(kernel, comm), out_shape=[jax.ShapeDtype...  30.5 us
    pallas_call x1, Pallas kernels, body(): pl.pallas_call(place, out_shape=[jax.ShapeDtypeStruct((N, R), F32)] * 2,...  1.98 us

profile of v3, /device:TPU:8, one launch (start us, length us, event | category | flops | bytes accessed | tf_op | source)
XLA Modules:
  0.0 33.1 jit_solution(18337251355140985960)
XLA Ops:
  0.6 30.5 %sgd_window.1 = (f32[1024,128]{1,0:T(8,128)}, f32[1024,128]{1,0:T(8,128)}) custom-call(s32[2,1024,1024]{2,1,0:T(8,128)} %inter.1, f32[1024,128]{1,0:T(8,128)} %users.1, f32[1024,128]{1,0:T(8,128)} %items.1), custom_call_target="tpu_custom_call" | custom-call | tf_op jit(solution)/shard_map/sgd_window/pallas_call | solution.py:334
  31.2 2.0 %place.1 = (f32[1024,128]{1,0:T(8,128)}, f32[1024,128]{1,0:T(8,128)}) custom-call(f32[1024,128]{1,0:T(8,128)} %get-tuple-element.4.users, f32[1024,128]{1,0:T(8,128)} %get-tuple-element.5.items), custom_call_target="tpu_custom_call" | custom-call | tf_op jit(solution)/shard_map/place/pallas_call | solution.py:378

commit v4 on v3

--- a/solution.py
+++ b/solution.py
@@ -14,20 +14,21 @@
 STEP = RATE * ALPHA
 N = 1024
 R = 128
-CHUNK = 256
+CHUNKS = (
+    ((0, 256), (256, 256), (512, 256), (768, 256)),
+    ((0, 256), (256, 256), (512, 256), (768, 256)),
+)
+LAST = len(CHUNKS[1])
+WIDEST = 256
 PARTS = 2
-CHUNKS = N // CHUNK
-ROWS = 256
-DROWS = 256
+ROWS = 512
+BLOCK = 256
 STEPS = (2, 1, 3)
 PAIRED_EARLY = [[], [], [], [(0, 0), (0, 1)]]
 PAIRED_ORDER = [[], [(0, 2), (0, 3), (1, 0), (1, 1)], [], [(1, 2), (1, 3)]]
-DIRECT_EARLY = [[], [], [], []]
-DIRECT_ORDER = [[(2, 0)], [(2, 1)], [(2, 2)], [(2, 3)]]
-KCAT = 1
-SKEW = 1
+DIRECT_EARLY = [[], [], [], [(2, 0)]]
+DIRECT_ORDER = [[(2, 1)], [(2, 2)], [(2, 3)], []]
 REPS = 8
-PIECE = CHUNK // REPS
 OTHERS = [(2, 1), (1, 1), (3, 1), (2, 0), (0, 1), (1, 0), (3, 0)]
 MESH = pl.DeviceIdType.MESH
 F32 = jnp.float32
@@ -70,8 +71,8 @@
         c.start()
     tiles = []
     for s in range(2):
-        for u in range(N // ROWS):
-            rows = pl.ds(u * ROWS, ROWS)
+        for u in range(N // BLOCK):
+            rows = pl.ds(u * BLOCK, BLOCK)
             t = pltpu.make_async_copy(inter.at[s, rows], tile.at[s, rows], tile_sem.at[s, u])
             if s == 0:
                 t.start()
@@ -86,47 +87,58 @@
             src_ref=src, dst_ref=dst, send_sem=send_sem, recv_sem=recv_sem,
             device_id=to, device_id_type=MESH)
 
+    def piece(c):
+        return CHUNKS[1][c][1] // REPS
+
     def rows_of(c, i, size):
-        return pl.ds(pl.multiple_of(c * CHUNK + i * size, size), size)
+        return pl.ds(pl.multiple_of(CHUNKS[1][c][0] + i * size, size), size)
 
     def scatter(c, k):
-        return remote(sent1.at[rows_of(c, ranks_to[k], PIECE)], parts.at[c, k],
+        p = piece(c)
+        return remote(sent1.at[rows_of(c, ranks_to[k], p)], parts.at[c, k, pl.ds(0, p)],
                       rs_send.at[c, k], rs_recv.at[c, k], (ranks_to[k], loop))
 
     def gather(c, k):
-        return remote(mean.at[c, pl.ds(0, PIECE)], item_out.at[rows_of(c, rep, PIECE)],
+        p = piece(c)
+        return remote(mean.at[c, pl.ds(0, p)], item_out.at[rows_of(c, rep, p)],
                       ag_send.at[c, k], ag_recv.at[c, k], (ranks_to[k], loop))
 
     def scatter_pair(c, k):
-        to = (y + STEPS[k]) % 4
-        return remote(sent1.at[rows_of(c, to, 2 * PIECE)], pairs.at[c, k],
+        to, p = (y + STEPS[k]) % 4, 2 * piece(c)
+        return remote(sent1.at[rows_of(c, to, p)], pairs.at[c, k, pl.ds(0, p)],
                       rs_send.at[c, k], rs_recv.at[c, k], (to * 2 + xh, loop))
 
     def swap_pair(c):
-        return remote(pair.at[c], other.at[c], x_send.at[c], x_recv.at[c], across)
+        p = pl.ds(0, 2 * piece(c))
+        return remote(pair.at[c, p], other.at[c, p], x_send.at[c], x_recv.at[c], across)
 
     def gather_pair(c, k):
-        return remote(mean.at[c], item_out.at[rows_of(c, y, 2 * PIECE)],
+        p = 2 * piece(c)
+        return remote(mean.at[c, pl.ds(0, p)], item_out.at[rows_of(c, y, p)],
                       ag_send.at[c, k], ag_recv.at[c, k], ((y + STEPS[k]) % 4 * 2 + xh, loop))
 
     def own_pair(c):
-        return pltpu.make_async_copy(mean.at[c], item_out.at[rows_of(c, y, 2 * PIECE)], own_sem.at[c])
+        p = 2 * piece(c)
+        return pltpu.make_async_copy(mean.at[c, pl.ds(0, p)], item_out.at[rows_of(c, y, p)], own_sem.at[c])
 
     def own(c):
-        return pltpu.make_async_copy(mean.at[c, pl.ds(0, PIECE)], item_out.at[rows_of(c, rep, PIECE)], own_sem.at[c])
+        p = piece(c)
+        return pltpu.make_async_copy(mean.at[c, pl.ds(0, p)], item_out.at[rows_of(c, rep, p)], own_sem.at[c])
 
     def along_y(c):
         for k in range(len(STEPS)):
             scatter_pair(c, k).wait_recv()
-        total = sent1[rows_of(c, y, 2 * PIECE), :]
+        p = 2 * piece(c)
+        total = sent1[rows_of(c, y, p), :]
         for k in range(len(STEPS)):
-            total = total + pairs[c, k]
-        pair[c] = total
+            total = total + pairs[c, k, 0:p]
+        pair[c, 0:p] = total
         swap_pair(c).start()
 
     def along_x(c):
         swap_pair(c).wait_recv()
-        mean[c] = (pair[c] + other[c]) * (1.0 / REPS)
+        p = 2 * piece(c)
+        mean[c, 0:p] = (pair[c, 0:p] + other[c, 0:p]) * (1.0 / REPS)
         for k in range(len(STEPS)):
             gather_pair(c, k).start()
         own_pair(c).start()
@@ -134,10 +146,11 @@
     def finish(c):
         for k in range(len(OTHERS)):
             scatter(c, k).wait_recv()
-        total = sent1[rows_of(c, rep, PIECE), :]
+        p = piece(c)
+        total = sent1[rows_of(c, rep, p), :]
         for k in range(len(OTHERS)):
-            total = total + parts[c, k]
-        mean[c, 0:PIECE] = total * (1.0 / REPS)
+            total = total + parts[c, k, 0:p]
+        mean[c, 0:p] = total * (1.0 / REPS)
         for k in range(len(OTHERS)):
             gather(c, k).start()
         own(c).start()
@@ -153,10 +166,9 @@
     for s in range(2):
         held = held0 if s == 0 else held1
         sent = sent0 if s == 0 else sent1
-        for u in range(N // ROWS):
-            rows = pl.ds(u * ROWS, ROWS)
-            block = uv[rows, :]
-            hi, lo = split(block)
+        for u in range(N // BLOCK):
+            rows = pl.ds(u * BLOCK, BLOCK)
+            hi, lo = split(uv[rows, :])
             ucat[rows, 0:R] = hi
             ucat[rows, R:2 * R] = lo
 
@@ -167,7 +179,7 @@
             utcat[R:2 * R, rows] = lo
 
         def prepare(c):
-            cols = pl.ds(c * CHUNK, CHUNK)
+            cols = pl.ds(*CHUNKS[s][c])
             h = held[cols, :]
             hi, lo = split(h)
             hnew[cols, 0:R] = hi
@@ -179,34 +191,30 @@
             hpred[3 * R:4 * R, cols] = lo
 
         def errors(c, u):
-            cols = pl.ds(c * CHUNK, CHUNK)
+            cols = pl.ds(*CHUNKS[s][c])
             rows = pl.ds(u * ROWS, ROWS)
             uc = ucat[rows, :]
-            if KCAT:
-                pred = dot(jnp.concatenate([uc, uc], 1), hpred[:, cols], NN)
-            else:
-                pred = dot(uc, hpred[0:2 * R, cols], NN) + dot(uc, hpred[2 * R:4 * R, cols], NN)
+            pred = dot(jnp.concatenate([uc, uc], 1), hpred[:, cols], NN)
             t = tile[s, rows, cols].astype(F32)
             hi, lo = split((1.0 / ALPHA + t) * (jnp.minimum(t, 1.0) - pred))
             ghi[rows, cols] = hi
             glo[rows, cols] = lo
 
         def gradient(c, u):
-            cols = pl.ds(c * CHUNK, CHUNK)
-            rows = pl.ds(u * DROWS, DROWS)
+            cols = pl.ds(*CHUNKS[s][c])
+            rows = pl.ds(u * ROWS, ROWS)
             ut = utcat[:, rows]
-            if KCAT:
-                d = dot(jnp.concatenate([ut, ut], 1), jnp.concatenate([ghi[rows, cols], glo[rows, cols]], 0), NN)
+            d = dot(jnp.concatenate([ut, ut], 1), jnp.concatenate([ghi[rows, cols], glo[rows, cols]], 0), NN)
+            width = CHUNKS[s][c][1]
+            if u == 0:
+                acc[:, 0:width] = d
             else:
-                d = dot(ut, ghi[rows, cols], NN) + dot(ut, glo[rows, cols], NN)
-            if u == 0:
-                acc[...] = d
-            else:
-                acc[...] += d
+                acc[:, 0:width] += d
 
         def update(c):
-            cols = pl.ds(c * CHUNK, CHUNK)
-            new = KEEP * held[cols, :] + STEP * (acc[0:R, :] + acc[R:2 * R, :]).T
+            cols = pl.ds(*CHUNKS[s][c])
+            width = CHUNKS[s][c][1]
+            new = KEEP * held[cols, :] + STEP * (acc[0:R, 0:width] + acc[R:2 * R, 0:width]).T
             sent[cols, :] = new
             if not comm:
                 if s == 0:
@@ -219,12 +227,13 @@
             if s == 0:
                 if c == 0:
                     pl.semaphore_wait(barrier, 1 + len(OTHERS))
-                cp = pltpu.make_async_remote_copy(
-                    src_ref=sent0.at[cols], dst_ref=held1.at[cols],
-                    send_sem=ring_send.at[c], recv_sem=ring_recv.at[c],
-                    device_id=after, device_id_type=MESH)
-                cp.start()
-                ring.append(cp)
+                first, width = CHUNKS[0][c]
+                for k, (at, size) in enumerate(CHUNKS[1]):
+                    if first <= at < first + width:
+                        rows = pl.ds(at, size)
+                        cp = remote(sent0.at[rows], held1.at[rows], ring_send.at[k], ring_recv.at[k], after)
+                        cp.start()
+                        ring.append(cp)
             else:
                 @pl.when(paired)
                 def _():
@@ -236,48 +245,46 @@
                     for k in range(len(OTHERS)):
                         scatter(c, k).start()
 
+        def arrive(u):
+            for i in range(u * ROWS // BLOCK, (u + 1) * ROWS // BLOCK):
+                tiles[s * (N // BLOCK) + i].wait()
+
         if s == 0:
             prepare(0)
-        if s == 0 and SKEW:
             for u in range(N // ROWS):
-                tiles[u].wait()
+                arrive(u)
                 errors(0, u)
                 turn(u)
-            for t in tiles[N // ROWS:]:
+            for t in tiles[N // BLOCK:]:
                 t.start()
-            for c in range(1, CHUNKS):
+            for c in range(1, len(CHUNKS[0])):
                 prepare(c)
                 for u in range(N // ROWS):
                     errors(c, u)
-                    if ROWS == DROWS:
-                        gradient(c - 1, u)
-                if ROWS != DROWS:
-                    for u in range(N // DROWS):
-                        gradient(c - 1, u)
+                    gradient(c - 1, u)
                 update(c - 1)
-            for u in range(N // DROWS):
-                gradient(CHUNKS - 1, u)
-            update(CHUNKS - 1)
+            for u in range(N // ROWS):
+                gradient(len(CHUNKS[0]) - 1, u)
+            update(len(CHUNKS[0]) - 1)
         else:
-            for c in range(CHUNKS):
-                if s == 1 and comm:
+            for c in range(LAST):
+                if comm:
                     ring[c].wait_recv()
-                if s == 1 or c > 0:
-                    prepare(c)
+                prepare(c)
                 for u in range(N // ROWS):
                     if c == 0:
-                        tiles[s * (N // ROWS) + u].wait()
+                        arrive(u)
                     errors(c, u)
                     if c == 0:
                         turn(u)
-                for u in range(N // DROWS):
+                for u in range(N // ROWS):
                     gradient(c, u)
                 update(c)
-                if comm and s == 1:
+                if comm:
                     go_on(PAIRED_EARLY[c], DIRECT_EARLY[c])
 
-        for u in range(N // ROWS):
-            rows = pl.ds(u * ROWS, ROWS)
+        for u in range(N // BLOCK):
+            rows = pl.ds(u * BLOCK, BLOCK)
             d = dot(ghi[rows, :], hnew[...], NN) + dot(glo[rows, :], hnew[...], NN)
             uv[rows, :] = KEEP * uv[rows, :] + STEP * (d[:, 0:R] + d[:, R:2 * R])
             if s == 1:
@@ -292,7 +299,7 @@
 
         @pl.when(paired)
         def _():
-            for c in range(CHUNKS):
+            for c in range(LAST):
                 swap_pair(c).wait_send()
                 own_pair(c).wait()
                 for k in range(len(STEPS)):
@@ -301,7 +308,7 @@
 
         @pl.when(jnp.logical_not(paired))
         def _():
-            for c in range(CHUNKS):
+            for c in range(LAST):
                 own(c).wait()
                 for k in range(len(OTHERS)):
                     scatter(c, k).wait_send()
@@ -349,24 +356,24 @@
             pltpu.VMEM((N, 2 * R), BF16),
             pltpu.VMEM((N, N), BF16),
             pltpu.VMEM((N, N), BF16),
-            pltpu.VMEM((2 * R, CHUNK), F32),
-            pltpu.VMEM((CHUNKS, n, PIECE, R), F32),
-            pltpu.VMEM((CHUNKS, len(STEPS), 2 * PIECE, R), F32),
-            pltpu.VMEM((CHUNKS, 2 * PIECE, R), F32),
-            pltpu.VMEM((CHUNKS, 2 * PIECE, R), F32),
-            pltpu.VMEM((CHUNKS, 2 * PIECE, R), F32),
+            pltpu.VMEM((2 * R, WIDEST), F32),
+            pltpu.VMEM((LAST, n, WIDEST // REPS, R), F32),
+            pltpu.VMEM((LAST, len(STEPS), 2 * WIDEST // REPS, R), F32),
+            pltpu.VMEM((LAST, 2 * WIDEST // REPS, R), F32),
+            pltpu.VMEM((LAST, 2 * WIDEST // REPS, R), F32),
+            pltpu.VMEM((LAST, 2 * WIDEST // REPS, R), F32),
             pltpu.SemaphoreType.DMA((2,)),
-            pltpu.SemaphoreType.DMA((2, N // ROWS)),
-            pltpu.SemaphoreType.DMA((N // ROWS,)),
-            pltpu.SemaphoreType.DMA((CHUNKS,)),
-            pltpu.SemaphoreType.DMA((CHUNKS,)),
-            pltpu.SemaphoreType.DMA((CHUNKS,)),
-            pltpu.SemaphoreType.DMA((CHUNKS, n)),
-            pltpu.SemaphoreType.DMA((CHUNKS, n)),
-            pltpu.SemaphoreType.DMA((CHUNKS,)),
-            pltpu.SemaphoreType.DMA((CHUNKS,)),
-            pltpu.SemaphoreType.DMA((CHUNKS, n)),
-            pltpu.SemaphoreType.DMA((CHUNKS, n)),
+            pltpu.SemaphoreType.DMA((2, N // BLOCK)),
+            pltpu.SemaphoreType.DMA((N // BLOCK,)),
+            pltpu.SemaphoreType.DMA((LAST,)),
+            pltpu.SemaphoreType.DMA((LAST,)),
+            pltpu.SemaphoreType.DMA((LAST,)),
+            pltpu.SemaphoreType.DMA((LAST, n)),
+            pltpu.SemaphoreType.DMA((LAST, n)),
+            pltpu.SemaphoreType.DMA((LAST,)),
+            pltpu.SemaphoreType.DMA((LAST,)),
+            pltpu.SemaphoreType.DMA((LAST, n)),
+            pltpu.SemaphoreType.DMA((LAST, n)),
         ],
         name="sgd_window",
         compiler_params=pltpu.CompilerParams(

time: 33.2 us -> 33 us (level)
  the two profiles are of different devices: /device:TPU:8 before, /device:TPU:4 now
where the time goes in v4:
time: 33 us; the launch traced here: 32.9 us
  Pallas kernels  32.3 us (98%)
  between operations  0.64 us (2%)
    pallas_call x1, Pallas kernels, body(): pl.pallas_call(functools.partial(kernel, comm), out_shape=[jax.ShapeDtype...  30.3 us
    pallas_call x1, Pallas kernels, body(): pl.pallas_call(place, out_shape=[jax.ShapeDtypeStruct((N, R), F32)] * 2,...  1.98 us

profile of v4, /device:TPU:4, one launch (start us, length us, event | category | flops | bytes accessed | tf_op | source)
XLA Modules:
  0.0 32.9 jit_solution(11086535909181672746)
XLA Ops:
  0.6 30.3 %sgd_window.1 = (f32[1024,128]{1,0:T(8,128)}, f32[1024,128]{1,0:T(8,128)}) custom-call(s32[2,1024,1024]{2,1,0:T(8,128)} %inter.1, f32[1024,128]{1,0:T(8,128)} %users.1, f32[1024,128]{1,0:T(8,128)} %items.1), custom_call_target="tpu_custom_call" | custom-call | tf_op jit(solution)/shard_map/sgd_window/pallas_call | solution.py:341
  30.9 2.0 %place.1 = (f32[1024,128]{1,0:T(8,128)}, f32[1024,128]{1,0:T(8,128)}) custom-call(f32[1024,128]{1,0:T(8,128)} %get-tuple-element.4.users, f32[1024,128]{1,0:T(8,128)} %get-tuple-element.5.items), custom_call_target="tpu_custom_call" | custom-call | tf_op jit(solution)/shard_map/place/pallas_call | solution.py:385
